TPU v7x, 512 devices: a whole 4x4x16 slice. The times are simulated.
512 devices in a mesh: group: 16 (over z_hi, y, core), blk: 32 (over z_lo, x).
Axes of the slice: x: 4, y: 4, z: 16 (z_hi: 2, z_lo: 8; z = z_hi * 8 + z_lo), core: 2. Of those that a mesh axis runs over, the one named last changes fastest.
Arguments:
- images: float32 [131072, 1152], P(('group', 'blk')), may hold values from -0.6 to 0.6
- held_text: float32 [131072, 1152], P(('group', 'blk')), may hold values from -0.6 to 0.6
- log_temp: float32 [1], replicated, may hold values from 1.6 to 2.6
- bias: float32 [1], replicated, may hold values from -4 to -1
Outputs:
- row_loss: float32 [131072], P(('group', 'blk'))
- image_grad: float32 [131072, 1152], P(('group', 'blk'))
- text_grad: float32 [131072, 1152], P(('group', 'blk'))
All inputs are finite; a program needn't handle non-finite values.
Results may differ from a plain program's by a relative error of at most 0.0001.
Values sent between devices are 32-bit elements; how exact they have to be, the bound alone decides.
A program may use at most 64 MiB of HBM per device.

v0:
```python
import math

import jax
import jax.numpy as jnp
from jax import lax
from jax.sharding import PartitionSpec as P


def from_behind(value, axis, steps):
    count = lax.axis_size(axis)
    pairs = [(source, (source + steps) % count) for source in range(count)]
    return lax.ppermute(value, axis, pairs)


def pairing(images, texts, scale, shift):
    logits = (
        scale
        * lax.dot_general(
            images,
            texts,
            (((1,), (1,)), ((), ())),
            precision=lax.Precision.HIGHEST,
            preferred_element_type=jnp.float32,
        )
        + shift
    )
    losses = jnp.sum(jax.nn.softplus(logits), axis=1)
    weights = jax.nn.sigmoid(logits) / jnp.float32(math.sqrt(4 * images.shape[0]))
    grad_x = scale * jnp.dot(
        weights, texts, precision=lax.Precision.HIGHEST, preferred_element_type=jnp.float32
    )
    grad_y = scale * lax.dot_general(
        weights,
        images,
        (((0,), (0,)), ((), ())),
        precision=lax.Precision.HIGHEST,
        preferred_element_type=jnp.float32,
    )
    return (losses, grad_x, grad_y)


def body(images, held_text, log_temp, bias):
    scale = jnp.exp(log_temp[0])
    shift = bias[0]
    rows = images.shape[0]
    losses, grad_x, own_y = pairing(images, held_text, scale, shift)

    def along_group(carried):
        return from_behind(carried, "blk", 1)

    carried = jnp.stack([held_text, own_y])
    for section in range(1, 4):
        if section == 2:
            carried = along_group(from_behind(carried, "group", 1))
        else:
            carried = along_group(carried)
        part_loss, part_x, part_y = pairing(images, carried[0], scale, shift)
        losses = losses + part_loss
        grad_x = grad_x + part_x
        carried = jnp.stack([carried[0], carried[1] + part_y])
    finished = from_behind(carried[1], "blk", -3)
    text_grad = from_behind(finished, "group", -1)
    row_loss = losses / jnp.float32(4 * rows)
    return (row_loss, grad_x, text_grad)


def solution(mesh):
    placed = (P(("group", "blk"), None), P(("group", "blk"), None), P(), P())
    return jax.shard_map(
        body,
        mesh=mesh,
        in_specs=placed,
        out_specs=(P(("group", "blk")), P(("group", "blk"), None), P(("group", "blk"), None)),
        check_vma=False,
    )
```

profile of v0, /device:TPU:153, one launch (start us, length us, event | category | flops | bytes accessed | tf_op | source)
XLA Modules:
  0.0 447.4 jit_solution(4868221527434873345)
XLA Ops:
  0.6 0.0 copy-start
  2.1 2.7 fusion.36
  4.8 1.3 fusion.2
  6.1 0.2 pad_maximum_fusion
  6.2 3.1 collective-permute-start
  9.3 54.2 %collective-permute-done = f32[2,256,1152]{2,1,0:T(8,128)S(1)} collective-permute-done((f32[2,256,1152]{2,1,0:T(8,128)S(1)}, f32[2,256,1152]{2,1,0:T(8,128)S(1)}, u32[]{:S(2)}, u32[]{:S(2)}) %collective-permute-start) | collective-permute-done | bytes 2359328 | tf_op jit(solution)/shard_map/ppermute | solution.py:12
  63.5 0.1 slice.26
  63.6 1.4 fusion.37
  65.0 1.3 fusion.7
  66.3 0.2 pad_maximum_fusion.1
  66.5 11.7 %collective-permute-start.1 = (f32[2,256,1152]{2,1,0:T(8,128)S(1)}, f32[2,256,1152]{2,1,0:T(8,128)S(1)}, u32[]{:S(2)}, u32[]{:S(2)}) collective-permute-start(f32[2,256,1152]{2,1,0:T(8,128)S(1)} %pad_maximum_fusion.1), channel_id=1, source_target_pairs={{0,32},{32,64},{64,96},{96,128},{128,160},{160,192},{192,224},{224... | collective-permute-start | bytes 7077896 | tf_op jit(solution)/shard_map/ppermute | solution.py:12
  78.2 65.2 %collective-permute-done.1 = f32[2,256,1152]{2,1,0:T(8,128)S(1)} collective-permute-done((f32[2,256,1152]{2,1,0:T(8,128)S(1)}, f32[2,256,1152]{2,1,0:T(8,128)S(1)}, u32[]{:S(2)}, u32[]{:S(2)}) %collective-permute-start.1) | collective-permute-done | bytes 2359328 | tf_op jit(solution)/shard_map/ppermute | solution.py:12
  143.4 21.6 %collective-permute-start.2 = (f32[2,256,1152]{2,1,0:T(8,128)S(1)}, f32[2,256,1152]{2,1,0:T(8,128)S(1)}, u32[]{:S(2)}, u32[]{:S(2)}) collective-permute-start(f32[2,256,1152]{2,1,0:T(8,128)S(1)} %collective-permute-done.1), channel_id=1, source_target_pairs={{0,1},{1,2},{2,3},{3,4},{4,5},{5,6},{6,7},{7,8},{8,9},{9,10},{10,1... | collective-permute-start | bytes 7077896 | tf_op jit(solution)/shard_map/ppermute | solution.py:12
  165.0 144.0 %collective-permute-done.2 = f32[2,256,1152]{2,1,0:T(8,128)S(1)} collective-permute-done((f32[2,256,1152]{2,1,0:T(8,128)S(1)}, f32[2,256,1152]{2,1,0:T(8,128)S(1)}, u32[]{:S(2)}, u32[]{:S(2)}) %collective-permute-start.2) | collective-permute-done | bytes 2359328 | tf_op jit(solution)/shard_map/ppermute | solution.py:12
  309.1 0.1 slice.28
  309.1 1.4 fusion.38
  310.5 1.3 fusion.5
  311.8 0.2 pad_maximum_fusion.2
  312.0 2.1 collective-permute-start.3
  314.1 30.8 %collective-permute-done.3 = f32[2,256,1152]{2,1,0:T(8,128)S(1)} collective-permute-done((f32[2,256,1152]{2,1,0:T(8,128)S(1)}, f32[2,256,1152]{2,1,0:T(8,128)S(1)}, u32[]{:S(2)}, u32[]{:S(2)}) %collective-permute-start.3) | collective-permute-done | bytes 2359328 | tf_op jit(solution)/shard_map/ppermute | solution.py:12
  344.9 1.4 fusion.39
  346.3 1.3 fusion.3
  347.6 1.9 collective-permute-start.4
  349.5 1.3 fusion.40
  350.8 14.9 %collective-permute-done.4 = f32[256,1152]{1,0:T(8,128)S(1)} collective-permute-done((f32[256,1152]{1,0:T(8,128)S(1)}, f32[256,1152]{1,0:T(8,128)S(1)}, u32[]{:S(2)}, u32[]{:S(2)}) %collective-permute-start.4) | collective-permute-done | bytes 1179680 | tf_op jit(solution)/shard_map/ppermute | solution.py:12
  365.8 1.9 collective-permute-start.5
  367.7 1.3 convolution_add_fusion.1
  369.0 0.6 add_multiply_fusion
  369.6 1.3 fusion.35
  370.8 2.4 fusion.1
  373.2 73.2 %collective-permute-done.5 = f32[256,1152]{1,0:T(8,128)S(1)} collective-permute-done((f32[256,1152]{1,0:T(8,128)S(1)}, f32[256,1152]{1,0:T(8,128)S(1)}, u32[]{:S(2)}, u32[]{:S(2)}) %collective-permute-start.5) | collective-permute-done | bytes 1179680 | tf_op jit(solution)/shard_map/ppermute | solution.py:12
  446.4 1.0 copy.12
  (3 shorter events, 0.0 us)
Async XLA Ops:
  0.6 1.4 copy-start
  4.7 1.3 copy-start.1
  6.2 57.3 %collective-permute-start = (f32[2,256,1152]{2,1,0:T(8,128)S(1)}, f32[2,256,1152]{2,1,0:T(8,128)S(1)}, u32[]{:S(2)}, u32[]{:S(2)}) collective-permute-start(f32[2,256,1152]{2,1,0:T(8,128)S(1)} %pad_maximum_fusion), channel_id=1, source_target_pairs={{0,1},{1,2},{2,3},{3,4},{4,5},{5,6},{6,7},{7,8},{8,9},{9,10},{10,1... | collective-permute-start | bytes 7077896 | tf_op jit(solution)/shard_map/ppermute | solution.py:12
  66.5 76.9 %collective-permute-start.1 = (f32[2,256,1152]{2,1,0:T(8,128)S(1)}, f32[2,256,1152]{2,1,0:T(8,128)S(1)}, u32[]{:S(2)}, u32[]{:S(2)}) collective-permute-start(f32[2,256,1152]{2,1,0:T(8,128)S(1)} %pad_maximum_fusion.1), channel_id=1, source_target_pairs={{0,32},{32,64},{64,96},{96,128},{128,160},{160,192},{192,224},{224... | collective-permute-start | bytes 7077896 | tf_op jit(solution)/shard_map/ppermute | solution.py:12
  143.4 165.6 %collective-permute-start.2 = (f32[2,256,1152]{2,1,0:T(8,128)S(1)}, f32[2,256,1152]{2,1,0:T(8,128)S(1)}, u32[]{:S(2)}, u32[]{:S(2)}) collective-permute-start(f32[2,256,1152]{2,1,0:T(8,128)S(1)} %collective-permute-done.1), channel_id=1, source_target_pairs={{0,1},{1,2},{2,3},{3,4},{4,5},{5,6},{6,7},{7,8},{8,9},{9,10},{10,1... | collective-permute-start | bytes 7077896 | tf_op jit(solution)/shard_map/ppermute | solution.py:12
  312.0 32.9 %collective-permute-start.3 = (f32[2,256,1152]{2,1,0:T(8,128)S(1)}, f32[2,256,1152]{2,1,0:T(8,128)S(1)}, u32[]{:S(2)}, u32[]{:S(2)}) collective-permute-start(f32[2,256,1152]{2,1,0:T(8,128)S(1)} %pad_maximum_fusion.2), channel_id=1, source_target_pairs={{0,1},{1,2},{2,3},{3,4},{4,5},{5,6},{6,7},{7,8},{8,9},{9,10},{10,1... | collective-permute-start | bytes 7077896 | tf_op jit(solution)/shard_map/ppermute | solution.py:12
  347.6 18.2 %collective-permute-start.4 = (f32[256,1152]{1,0:T(8,128)S(1)}, f32[256,1152]{1,0:T(8,128)S(1)}, u32[]{:S(2)}, u32[]{:S(2)}) collective-permute-start(f32[256,1152]{1,0:T(8,128)S(1)} %fusion.3), channel_id=1, source_target_pairs={{0,29},{1,30},{2,31},{3,0},{4,1},{5,2},{6,3},{7,4},{8,5},{9,6},{10... | collective-permute-start | bytes 3538952 | tf_op jit(solution)/shard_map/ppermute | solution.py:12
  365.8 80.6 %collective-permute-start.5 = (f32[256,1152]{1,0:T(8,128)S(1)}, f32[256,1152]{1,0:T(8,128)S(1)}, u32[]{:S(2)}, u32[]{:S(2)}) collective-permute-start(f32[256,1152]{1,0:T(8,128)S(1)} %collective-permute-done.4), channel_id=1, source_target_pairs={{0,480},{32,0},{64,32},{96,64},{128,96},{160,128},{192,160},{224,1... | collective-permute-start | bytes 3538952 | tf_op jit(solution)/shard_map/ppermute | solution.py:12
where the time goes:
time: 448 us; the launch traced here: 447 us
  waiting for transfers between devices  382 us (85%)
  starting transfers between devices  42.3 us (9%)
  matrix products  18.3 us (4%)
    ppermute x6, waiting for transfers between devices, from_behind(): return lax.ppermute(value, axis, pairs)  382 us
    ppermute x6, starting transfers between devices, from_behind(): return lax.ppermute(value, axis, pairs)  42.3 us
  transfers between devices with their start and end apart: 6, of which 6 were waited for; matrix products, arithmetic and copies ran while one was open for 2% of the time, Pallas kernels for 0%

commit v1 on v0

v1 whole, which is shorter than its diff:
```python
import functools
import math

import jax
import jax.numpy as jnp
from jax import lax
from jax.experimental import pallas as pl
from jax.experimental.pallas import tpu as pltpu
from jax.sharding import PartitionSpec as P

F32, BF16 = jnp.float32, jnp.bfloat16
MESH = pl.DeviceIdType.MESH
NT = (((1,), (1,)), ((), ()))
NN = (((1,), (0,)), ((), ()))
PARTS = 4


def split(value):
    high = value.astype(BF16)
    return high, (value - high.astype(F32)).astype(BF16)


def dot3(a, b, dims):
    def one(p, q):
        return lax.dot_general(p, q, dims, preferred_element_type=F32)

    return one(a[0], b[0]) + (one(a[0], b[1]) + one(a[1], b[0]))


def device(group, blk):
    return {"group": lax.rem(group + 16, 16), "blk": lax.rem(blk + 32, 32)}


def at(x, y, z, core):
    z_hi, z_lo = z // 8, lax.rem(z, 8)
    return {"group": z_hi * 8 + y * 2 + core, "blk": z_lo * 4 + lax.rem(x + 4, 4)}


def kernel(
    temp_ref, bias_ref, x_hbm, y_hbm, loss_ref, gx_hbm, gy_hbm,
    x_in, y_in, y_far, x_far, xh, xl, yh, yl, wt, gx_own, gy_own, gx_far, gy_far,
    gx_back, gy_back, relay_a, relay_b, loss_part, loss_far, loss_back,
    load_sem, send_sem, recv_sem, out_sem,
):
    rows, width = x_in.shape
    part = rows // PARTS
    group, blk = lax.axis_index("group"), lax.axis_index("blk")
    x, z = lax.rem(blk, 4), (group // 8) * 8 + blk // 4
    y, core = lax.rem(group // 2, 4), lax.rem(group, 2)
    first = lax.rem(group, 8) == 0
    last = lax.rem(group, 8) == 7

    next_blk, prev_blk = device(group, blk + 1), device(group, blk - 1)
    ahead, behind = device(group + 1, blk + 2), device(group - 1, blk - 2)

    def relay_a_at(j):
        return at(x + 2, j, z, 1)

    def relay_b_at(j):
        return at(x, j, z, 0)

    a_from = at(x + 2, 0, z, 0)
    a_to = device(a_from["group"] - 1, a_from["blk"] - 2)
    b_from = at(x, 3, z, 1)
    b_to = device(b_from["group"] + 1, b_from["blk"] + 2)

    def rows_of(j):
        return pl.ds(pl.multiple_of(j * part, part), part)

    def load(k, source, target):
        return pltpu.make_async_copy(source, target, load_sem.at[k])

    load(0, x_hbm, x_in).start()
    load(1, y_hbm, y_in).start()

    barrier = pltpu.get_barrier_semaphore()

    def signal(to):
        pl.semaphore_signal(barrier, inc=1, device_id=to, device_id_type=MESH)

    signal(prev_blk)
    signal(next_blk)

    @pl.when(jnp.logical_not(last))
    def _():
        signal(ahead)

    @pl.when(last)
    def _():
        src = device(group + 1, blk + 2)
        z_src = (src["group"] // 8) * 8 + src["blk"] // 4
        for j in range(PARTS):
            signal(at(lax.rem(src["blk"], 4) + 2, j, z_src, 1))

    @pl.when(jnp.logical_not(first))
    def _():
        signal(behind)

    @pl.when(first)
    def _():
        src = device(group - 1, blk - 2)
        z_src = (src["group"] // 8) * 8 + src["blk"] // 4
        for j in range(PARTS):
            signal(at(lax.rem(src["blk"], 4), j, z_src, 0))
        signal(behind)

    @pl.when(core == 1)
    def _():
        signal(a_from)

    @pl.when(core == 0)
    def _():
        signal(b_from)

    pl.semaphore_wait(barrier, jnp.where(first, PARTS + 4, jnp.where(last, PARTS + 5, 5)))

    def remote(k, source, target, to):
        return pltpu.make_async_remote_copy(
            src_ref=source, dst_ref=target, send_sem=send_sem.at[k], recv_sem=recv_sem.at[k],
            device_id=to, device_id_type=MESH,
        )

    def x_copy(j, to):
        return remote(j, x_hbm.at[rows_of(j)], x_far.at[rows_of(j)], to)

    def x_to_relay(j):
        return pltpu.make_async_remote_copy(
            src_ref=x_hbm.at[rows_of(j)], dst_ref=relay_a, send_sem=send_sem.at[j], recv_sem=recv_sem.at[14],
            device_id=relay_a_at(j), device_id_type=MESH,
        )

    def a_hand_on():
        return pltpu.make_async_remote_copy(
            src_ref=relay_a, dst_ref=x_far.at[rows_of(y)], send_sem=send_sem.at[14], recv_sem=recv_sem.at[y],
            device_id=a_to, device_id_type=MESH,
        )

    def gx_copy(j, to):
        return remote(4 + j, gx_far.at[rows_of(j)], gx_back.at[rows_of(j)], to)

    def gx_to_relay(j):
        return pltpu.make_async_remote_copy(
            src_ref=gx_far.at[rows_of(j)], dst_ref=relay_b, send_sem=send_sem.at[4 + j], recv_sem=recv_sem.at[15],
            device_id=relay_b_at(j), device_id_type=MESH,
        )

    def b_hand_on():
        return pltpu.make_async_remote_copy(
            src_ref=relay_b, dst_ref=gx_back.at[rows_of(y)], send_sem=send_sem.at[15], recv_sem=recv_sem.at[4 + y],
            device_id=b_to, device_id_type=MESH,
        )

    def gy_copy(j):
        return remote(8 + j, gy_far.at[rows_of(j)], gy_back.at[rows_of(j)], prev_blk)

    y_copy = remote(12, y_hbm, y_far, next_blk)
    loss_copy = remote(13, loss_far, loss_back, ahead)

    @pl.when(first)
    def _():
        for j in range(PARTS):
            x_to_relay(j).start()

    y_copy.start()

    @pl.when(jnp.logical_not(first))
    def _():
        for j in range(PARTS):
            x_copy(j, behind).start()

    @pl.when(core == 1)
    def _():
        x_to_relay(0).wait_recv()
        a_hand_on().start()

    scale = jnp.exp(jnp.full((1, rows), temp_ref[0], F32))
    shift = bias_ref[0]
    gain = scale * (1.0 / math.sqrt(4 * rows))

    def pair(products):
        logits = scale * products + shift
        small = jnp.exp(-jnp.abs(logits))
        total = 1.0 + small
        log1p = jnp.where(total == 1.0, small, jnp.log(total) * (small / (total - 1.0)))
        weights = jnp.where(logits >= 0, 1.0, small) / total
        return jnp.maximum(logits, 0.0) + log1p, weights * gain

    def lanes(losses):
        return losses[:, :128] + losses[:, 128:]

    def both(high, low, k, where=slice(None)):
        return high[k, where], low[k, where]

    def split_block(source, k, high, low):
        def step(j, _):
            high[k, rows_of(j)], low[k, rows_of(j)] = split(source[rows_of(j)])
            return 0

        lax.fori_loop(0, PARTS, step, 0)

    load(0, x_hbm, x_in).wait()
    split_block(x_in, 0, xh, xl)
    load(1, y_hbm, y_in).wait()
    split_block(y_in, 0, yh, yl)
    losses, weights = pair(dot3(both(xh, xl, 0), both(yh, yl, 0), NT))
    loss_part[...] = lanes(losses)
    gx_own[...] = dot3(split(weights), both(yh, yl, 0), NN)
    gy_own[...] = dot3(split(weights.T), both(xh, xl, 0), NN)

    y_copy.wait_recv()
    split_block(y_far, 1, yh, yl)
    losses, weights = pair(dot3(both(xh, xl, 0), both(yh, yl, 1), NT))
    loss_part[...] += lanes(losses)
    gx_own[...] += dot3(split(weights), both(yh, yl, 1), NN)
    gy_far[...] = dot3(split(weights.T), both(xh, xl, 0), NN)

    def far_step(j, _):
        x_copy(j, behind).wait_recv()
        here = rows_of(j)
        xh[1, here], xl[1, here] = split(x_far[here])
        image = both(xh, xl, 1, here)
        losses, weights = pair(dot3(image, both(yh, yl, 0), NT))
        loss_far[here] = lanes(losses)
        wt[0, here] = weights
        grad = dot3(split(weights), both(yh, yl, 0), NN)
        losses, weights = pair(dot3(image, both(yh, yl, 1), NT))
        loss_far[here] += lanes(losses)
        wt[1, here] = weights
        gx_far[here] = grad + dot3(split(weights), both(yh, yl, 1), NN)

        @pl.when(last)
        def _():
            gx_to_relay(j).start()

        @pl.when(jnp.logical_not(last))
        def _():
            gx_copy(j, ahead).start()

        return 0

    lax.fori_loop(0, PARTS, far_step, 0)
    loss_copy.start()

    wt[1] = wt[1].T

    def text_step(j, _):
        here = rows_of(j)
        gy_far[here] += dot3(split(wt[1, here]), both(xh, xl, 1), NN)
        gy_copy(j).start()
        return 0

    lax.fori_loop(0, PARTS, text_step, 0)

    @pl.when(core == 0)
    def _():
        gx_to_relay(0).wait_recv()
        b_hand_on().start()

    gy_own[...] += dot3(split(wt[0].T), both(xh, xl, 1), NN)

    def out(k, j, source, target):
        return pltpu.make_async_copy(source.at[rows_of(j)], target.at[rows_of(j)], out_sem.at[4 * k + j])

    for j in range(PARTS):
        gy_copy(j).wait_recv()
        gy_own[rows_of(j)] += gy_back[rows_of(j)]
        out(1, j, gy_own, gy_hbm).start()
    for j in range(PARTS):
        gx_copy(j, ahead).wait_recv()
        gx_own[rows_of(j)] += gx_back[rows_of(j)]
        out(0, j, gx_own, gx_hbm).start()
    loss_copy.wait_recv()
    sums = lax.dot_general(
        jnp.ones((8, 128), F32), loss_part[...] + loss_back[...], NT,
        precision=lax.Precision.HIGHEST, preferred_element_type=F32,
    )
    loss_ref[...] = sums * (1.0 / (4 * rows))

    y_copy.wait_send()
    loss_copy.wait_send()
    for j in range(PARTS):
        x_copy(j, behind).wait_send()
        gx_copy(j, ahead).wait_send()
        gy_copy(j).wait_send()

    @pl.when(core == 1)
    def _():
        a_hand_on().wait_send()

    @pl.when(core == 0)
    def _():
        b_hand_on().wait_send()

    for j in range(PARTS):
        out(1, j, gy_own, gy_hbm).wait()
        out(0, j, gx_own, gx_hbm).wait()


def body(images, held_text, log_temp, bias):
    rows, width = images.shape
    block = pltpu.VMEM((rows, width), F32)
    halves = pltpu.VMEM((2, rows, width), BF16)
    relay = pltpu.VMEM((rows // PARTS, width), F32)
    loss = pltpu.VMEM((rows, 128), F32)
    anywhere = pl.BlockSpec(memory_space=pl.ANY)
    scalar = pl.BlockSpec(memory_space=pltpu.SMEM)
    whole = jax.ShapeDtypeStruct((rows, width), F32)
    row_loss, grad_x, grad_y = pl.pallas_call(
        kernel,
        out_shape=(jax.ShapeDtypeStruct((8, rows), F32), whole, whole),
        in_specs=[scalar, scalar, anywhere, anywhere],
        out_specs=(pl.BlockSpec(memory_space=pltpu.VMEM), anywhere, anywhere),
        scratch_shapes=[
            block, block, block, block, halves, halves, halves, halves,
            pltpu.VMEM((2, rows, rows), F32),
            block, block, block, block, block, block, relay, relay, loss, loss, loss,
            pltpu.SemaphoreType.DMA((2,)),
            pltpu.SemaphoreType.DMA((16,)),
            pltpu.SemaphoreType.DMA((16,)),
            pltpu.SemaphoreType.DMA((8,)),
        ],
        compiler_params=pltpu.CompilerParams(
            collective_id=0, has_side_effects=True, vmem_limit_bytes=48 * 1024 * 1024
        ),
        name="pair_tiles",
    )(log_temp, bias, images, held_text)
    return row_loss[0], grad_x, grad_y


def solution(mesh):
    placed = (P(("group", "blk"), None), P(("group", "blk"), None), P(), P())
    return jax.shard_map(
        body,
        mesh=mesh,
        in_specs=placed,
        out_specs=(P(("group", "blk")), P(("group", "blk"), None), P(("group", "blk"), None)),
        check_vma=False,
    )
```

time: 448 us -> 165 us (0.37)
  the two profiles are of different devices: /device:TPU:153 before, /device:TPU:8 now
where the time goes in v1:
time: 165 us
  Pallas kernels  158 us (96%)
  local copies, waits for them, and re-layouts  5.12 us (3%)
  between operations  1.94 us (1%)
    pallas_call x1, Pallas kernels, body(): pl.pallas_call(kernel, out_shape=(jax.ShapeDtypeStruct((8, rows), F32), w...  158 us
    unnamed x6, local copies, waits for them, and re-layouts  4.56 us

profile of v1, /device:TPU:8, one launch (start us, length us, event | category | flops | bytes accessed | tf_op | source)
XLA Modules:
  0.0 165.3 jit_solution(3504703092754596429)
XLA Ops:
  1.9 0.0 copy-start
  1.9 1.3 copy-done
  3.2 0.0 copy-start.1
  3.2 1.3 copy-done.1
  4.5 158.2 %pair_tiles.1 = (f32[8,256]{1,0:T(8,128)S(1)}, f32[256,1152]{1,0:T(8,128)S(1)}, f32[256,1152]{1,0:T(8,128)S(1)}) custom-call(f32[1]{0:T(128)S(6)} %copy.9.temp_ref, f32[1]{0:T(128)S(6)} %copy.10.bias_ref, f32[256,1152]{1,0:T(8,128)S(1)} %copy-done, f32[256,1152]{1,0:T(8,128)S(1)} %copy-done.1), custom_call_target="tpu_custom_call" | custom-call | tf_op jit(solution)/shard_map/pair_tiles/pallas_call | solution.py:308
  162.7 0.6 slice.3
  163.2 1.0 copy.11
  164.2 1.0 copy.12
Async XLA Ops:
  1.9 1.3 copy-start
  3.2 1.3 copy-start.1

commit v2 on v0

v2 whole, which is shorter than its diff:
```python
import math

import jax
import jax.numpy as jnp
from jax import lax
from jax.experimental import pallas as pl
from jax.experimental.pallas import tpu as pltpu
from jax.sharding import PartitionSpec as P

F32, BF16 = jnp.float32, jnp.bfloat16
MESH = pl.DeviceIdType.MESH
NT = (((1,), (1,)), ((), ()))
NN = (((1,), (0,)), ((), ()))
PARTS = 4


def split(value):
    high = value.astype(BF16)
    return high, (value - high.astype(F32)).astype(BF16)


def dot3(a, b, dims):
    def one(p, q):
        return lax.dot_general(p, q, dims, preferred_element_type=F32)

    return one(a[0], b[0]) + (one(a[0], b[1]) + one(a[1], b[0]))


def device(group, blk):
    return {"group": lax.rem(group + 16, 16), "blk": lax.rem(blk + 32, 32)}


def at(x, y, z, core):
    return {"group": (z // 8) * 8 + y * 2 + core, "blk": lax.rem(z, 8) * 4 + x}


def kernel(
    temp_ref, bias_ref, x_hbm, y_hbm, loss_ref, gx_hbm, gy_hbm,
    own, own_high, own_low, far, high, low, grad, relay, loss_part,
    load_sem, send_sem, recv_sem, out_sem,
):
    rows = own.shape[1]
    part = rows // PARTS
    group, blk = lax.axis_index("group"), lax.axis_index("blk")
    x, z = lax.rem(blk, 4), (group // 8) * 8 + blk // 4
    y, core = lax.rem(group // 2, 4), lax.rem(group, 2)
    first = lax.rem(group, 8) == 0
    last = lax.rem(group, 8) == 7
    edge = first | last
    near = jnp.where(first, 1, 0)
    late = 1 - near
    relays = (x == 1) | (x == 2)

    def step(kind):
        return 1 - 2 * kind

    def along(kind):
        return device(group, blk + step(kind))

    def across(kind):
        return device(group + step(kind), blk + step(kind))

    def ring(x_from):
        return jnp.where(x_from >= 2, 2, 1)

    def relay_of(kind, holder, j):
        z_from = (holder["group"] // 8) * 8 + holder["blk"] // 4
        return at(ring(lax.rem(holder["blk"], 4)), j, z_from, kind)

    def served(slot):
        z_hi, z_lo = z // 8, lax.rem(z, 8)
        return device(z_hi * 8 + jnp.where(core == 0, 7, 0), z_lo * 4 + 2 * (x - 1) + slot)

    def rows_of(j):
        return pl.ds(pl.multiple_of(j * part, part), part)

    load_x = pltpu.make_async_copy(x_hbm, own.at[1], load_sem.at[1])
    load_y = pltpu.make_async_copy(y_hbm, own.at[0], load_sem.at[0])
    load_y.start()
    load_x.start()

    barrier = pltpu.get_barrier_semaphore()

    def signal(to):
        pl.semaphore_signal(barrier, inc=1, device_id=to, device_id_type=MESH)

    signal(along(0))
    signal(along(1))

    @pl.when(jnp.logical_not(first))
    def _():
        signal(across(1))

    @pl.when(jnp.logical_not(last))
    def _():
        signal(across(0))

    @pl.when(edge)
    def _():
        holder = device(group - step(late), blk - 2 * step(late))
        for j in range(PARTS):
            signal(relay_of(late, holder, j))

    @pl.when(relays)
    def _():
        signal(served(0))
        signal(served(1))

    pl.semaphore_wait(barrier, jnp.where(edge, PARTS + 3, 4) + jnp.where(relays, 2, 0))
    load_y.wait()
    load_x.wait()

    def copy(kind, leg, j, source, to):
        k = kind * 12 + leg * 4 + j
        return pltpu.make_async_remote_copy(
            src_ref=source, dst_ref=far.at[kind, leg, rows_of(j)], send_sem=send_sem.at[k], recv_sem=recv_sem.at[k],
            device_id=to, device_id_type=MESH,
        )

    def leg0(kind, j):
        return copy(kind, 0, j, own.at[kind, rows_of(j)], along(kind))

    def leg1(kind, j):
        return copy(kind, 1, j, far.at[kind, 0, rows_of(j)], across(kind))

    def leg2(kind, j):
        return copy(kind, 2, j, far.at[kind, 1, rows_of(j)], along(kind))

    def to_relay(j):
        me = {"group": group, "blk": blk}
        return pltpu.make_async_remote_copy(
            src_ref=own.at[near, rows_of(j)], dst_ref=relay.at[lax.rem(x, 2)],
            send_sem=send_sem.at[near * 12 + 4 + j], recv_sem=recv_sem.at[24 + lax.rem(x, 2)],
            device_id=relay_of(near, me, j), device_id_type=MESH,
        )

    def from_relay(slot):
        holder = served(slot)
        return pltpu.make_async_remote_copy(
            src_ref=relay.at[slot], dst_ref=far.at[core, 1, rows_of(y)],
            send_sem=send_sem.at[24 + slot], recv_sem=recv_sem.at[core * 12 + 4 + y],
            device_id=device(holder["group"] + step(core), holder["blk"] + 2 * step(core)), device_id_type=MESH,
        )

    def relay_in(slot):
        return pltpu.make_async_remote_copy(
            src_ref=own.at[0, rows_of(0)], dst_ref=relay.at[slot],
            send_sem=send_sem.at[24 + slot], recv_sem=recv_sem.at[24 + slot],
            device_id=along(0), device_id_type=MESH,
        )

    @pl.when(edge)
    def _():
        for j in range(PARTS):
            to_relay(j).start()

    for j in range(2):
        for kind in range(2):
            leg0(kind, j).start()

    scale = jnp.exp(jnp.full((1, rows), temp_ref[0], F32))
    shift = bias_ref[0]
    gain = scale * (1.0 / math.sqrt(4 * rows))

    def pair(products):
        logits = scale * products + shift
        small = jnp.exp(-jnp.abs(logits))
        total = 1.0 + small
        log1p = jnp.where(total == 1.0, small, jnp.log(total) * (small / (total - 1.0)))
        weights = jnp.where(logits >= 0, 1.0, small) / total
        losses = jnp.maximum(logits, 0.0) + log1p
        return losses[:, :128] + losses[:, 128:], weights * gain

    def held(kind):
        return own_high[kind], own_low[kind]

    def own_part(j, _):
        here = rows_of(j)
        for kind in range(2):
            own_high[kind, here], own_low[kind, here] = split(own[kind, here])
        return 0

    lax.fori_loop(0, PARTS, own_part, 0)

    losses, weights = pair(dot3(held(1), held(0), NT))
    loss_part[0] = losses
    grad[0] = dot3(split(weights), held(0), NN)
    grad[1] = dot3(split(weights.T), held(1), NN)

    def meet(kind, leg):
        def part_of(j, _):
            here = rows_of(j)
            high[here], low[here] = split(far[kind, leg, here])
            return 0

        lax.fori_loop(0, PARTS, part_of, 0)
        other = (high[...], low[...])
        mine = 1 - kind
        losses, weights = pair(dot3((own_high[mine], own_low[mine]), other, NT))
        loss_part[kind] += losses
        grad[kind] += dot3(split(weights), other, NN)

    loss_part[1] = jnp.zeros_like(loss_part[1])

    def take0(j):
        for kind in range(2):
            leg0(kind, j).wait_recv()

            @pl.when(jnp.logical_not(edge & (near == kind)))
            def _():
                leg1(kind, j).start()

            leg0(kind, j).wait_send()
            if j + 2 < PARTS:
                leg0(kind, j + 2).start()

    def take1(kind, j):
        leg1(kind, j).wait_recv()
        leg2(kind, j).start()

    def take1_ordinary(j):
        @pl.when(edge)
        def _():
            take1(near, j)

        @pl.when(jnp.logical_not(edge))
        def _():
            take1(0, j)
            take1(1, j)

    take0(0)
    take0(1)

    @pl.when(relays)
    def _():
        for slot in range(2):
            relay_in(slot).wait_recv()
            from_relay(slot).start()

    take1_ordinary(0)
    take0(2)
    take1_ordinary(1)
    take0(3)
    meet(0, 0)
    take1_ordinary(2)
    meet(1, 0)
    take1_ordinary(3)
    meet(near, 1)

    @pl.when(edge)
    def _():
        for j in range(PARTS):
            take1(late, j)

    meet(late, 1)
    for j in range(PARTS):
        leg2(near, j).wait_recv()
    meet(near, 2)

    write_x = pltpu.make_async_copy(grad.at[0], gx_hbm, out_sem.at[0])
    write_y = pltpu.make_async_copy(grad.at[1], gy_hbm, out_sem.at[1])

    @pl.when(first)
    def _():
        write_y.start()

    @pl.when(jnp.logical_not(first))
    def _():
        write_x.start()

    for j in range(PARTS):
        leg2(late, j).wait_recv()
    meet(late, 2)

    @pl.when(first)
    def _():
        write_x.start()

    @pl.when(jnp.logical_not(first))
    def _():
        write_y.start()

    loss_ref[...] = lax.dot_general(
        jnp.ones((8, 128), F32), loss_part[0], NT, precision=lax.Precision.HIGHEST, preferred_element_type=F32
    ) * (1.0 / (4 * rows))

    for kind in range(2):
        for j in range(PARTS):
            leg1(kind, j).wait_send()
            leg2(kind, j).wait_send()

    @pl.when(relays)
    def _():
        from_relay(0).wait_send()
        from_relay(1).wait_send()

    write_x.wait()
    write_y.wait()


def body(images, held_text, log_temp, bias):
    rows, width = images.shape
    pieces = pltpu.VMEM((2, rows, width), F32)
    halves = pltpu.VMEM((2, rows, width), BF16)
    half = pltpu.VMEM((rows, width), BF16)
    in_hbm = pl.BlockSpec(memory_space=pltpu.HBM)
    scalar = pl.BlockSpec(memory_space=pltpu.SMEM)
    whole = jax.ShapeDtypeStruct((rows, width), F32)
    row_loss, grad_x, grad_y = pl.pallas_call(
        kernel,
        out_shape=(jax.ShapeDtypeStruct((8, rows), F32), whole, whole),
        in_specs=[scalar, scalar, in_hbm, in_hbm],
        out_specs=(pl.BlockSpec(memory_space=pltpu.VMEM), in_hbm, in_hbm),
        scratch_shapes=[
            pieces, halves, halves,
            pltpu.VMEM((2, 3, rows, width), F32),
            half, half, pieces,
            pltpu.VMEM((2, rows // PARTS, width), F32),
            pltpu.VMEM((2, rows, 128), F32),
            pltpu.SemaphoreType.DMA((2,)),
            pltpu.SemaphoreType.DMA((26,)),
            pltpu.SemaphoreType.DMA((26,)),
            pltpu.SemaphoreType.DMA((2,)),
        ],
        compiler_params=pltpu.CompilerParams(
            collective_id=0, has_side_effects=True, vmem_limit_bytes=60 * 1024 * 1024
        ),
        name="pair_tiles",
    )(log_temp, bias, images, held_text)
    return row_loss[0], grad_x, grad_y


def solution(mesh):
    placed = (P(("group", "blk"), None), P(("group", "blk"), None), P(), P())
    return jax.shard_map(
        body,
        mesh=mesh,
        in_specs=placed,
        out_specs=(P(("group", "blk")), P(("group", "blk"), None), P(("group", "blk"), None)),
        check_vma=False,
    )
```

time: 448 us -> 136 us (0.30)
  the two profiles are of different devices: /device:TPU:153 before, /device:TPU:32 now
where the time goes in v2:
time: 136 us
  Pallas kernels  129 us (95%)
  local copies, waits for them, and re-layouts  4.73 us (3%)
  between operations  1.93 us (1%)
    pallas_call x1, Pallas kernels, body(): pl.pallas_call(kernel, out_shape=(jax.ShapeDtypeStruct((8, rows), F32), w...  129 us
    unnamed x4, local copies, waits for them, and re-layouts  3.47 us

profile of v2, /device:TPU:32, one launch (start us, length us, event | category | flops | bytes accessed | tf_op | source)
XLA Modules:
  0.0 135.9 jit_solution(16482473084375582565)
XLA Ops:
  1.9 129.3 %pair_tiles.1 = (f32[8,256]{1,0:T(8,128)}, f32[256,1152]{1,0:T(8,128)}, f32[256,1152]{1,0:T(8,128)}) custom-call(f32[1]{0:T(128)S(6)} %copy.9.temp_ref, f32[1]{0:T(128)S(6)} %copy.10.bias_ref, f32[256,1152]{1,0:T(8,128)} %x_hbm.1, f32[256,1152]{1,0:T(8,128)} %y_hbm.1), custom_call_target="tpu_custom_call" | custom-call | tf_op jit(solution)/shard_map/pair_tiles/pallas_call | solution.py:309
  131.2 1.3 slice.3
  132.4 0.0 copy-start
  132.4 2.5 %copy.11 = f32[256,1152]{1,0:T(8,128)} copy(f32[256,1152]{1,0:T(8,128)} %get-tuple-element.13) | data formatting | bytes 2359296
  134.9 0.0 copy-done
  134.9 1.0 copy.12
Async XLA Ops:
  132.4 2.5 %copy-start = (f32[256,1152]{1,0:T(8,128)S(1)}, f32[256,1152]{1,0:T(8,128)}, u32[]{:S(2)}) copy-start(f32[256,1152]{1,0:T(8,128)} %get-tuple-element.14) | copy-start | bytes 3538948

commit v3 on v2

--- a/solution.py
+++ b/solution.py
@@ -49,7 +49,8 @@
     edge = first | last
     near = jnp.where(first, 1, 0)
     late = 1 - near
-    relays = (x == 1) | (x == 2)
+    inner = (x == 1) | (x == 2)
+    outer = jnp.logical_not(inner)
 
     def step(kind):
         return 1 - 2 * kind
@@ -61,15 +62,17 @@
         return device(group + step(kind), blk + step(kind))
 
     def ring(x_from):
-        return jnp.where(x_from >= 2, 2, 1)
+        return jnp.where(x_from == 0, 2, jnp.where(x_from == 3, 1, x_from))
 
     def relay_of(kind, holder, j):
         z_from = (holder["group"] // 8) * 8 + holder["blk"] // 4
         return at(ring(lax.rem(holder["blk"], 4)), j, z_from, kind)
 
     def served(slot):
-        z_hi, z_lo = z // 8, lax.rem(z, 8)
-        return device(z_hi * 8 + jnp.where(core == 0, 7, 0), z_lo * 4 + 2 * (x - 1) + slot)
+        x_from = x if slot == 0 else jnp.where(x == 2, 0, 3)
+        return at(x_from, jnp.where(core == 0, 3, 0), z, 1 - core)
+
+    pass_to, pass_from = at(ring(x), y, z, core), at(jnp.where(x == 2, 0, 3), y, z, core)
 
     def rows_of(j):
         return pl.ds(pl.multiple_of(j * part, part), part)
@@ -101,12 +104,13 @@
         for j in range(PARTS):
             signal(relay_of(late, holder, j))
 
-    @pl.when(relays)
-    def _():
-        signal(served(0))
-        signal(served(1))
-
-    pl.semaphore_wait(barrier, jnp.where(edge, PARTS + 3, 4) + jnp.where(relays, 2, 0))
+    signal(served(0))
+
+    @pl.when(inner)
+    def _():
+        signal(pass_from)
+
+    pl.semaphore_wait(barrier, jnp.where(edge, PARTS + 3, 4) + jnp.where(inner, 2, 1))
     load_y.wait()
     load_x.wait()
 
@@ -126,28 +130,22 @@
     def leg2(kind, j):
         return copy(kind, 2, j, far.at[kind, 1, rows_of(j)], along(kind))
 
+    def hop(source, target, k_send, k_recv, to):
+        return pltpu.make_async_remote_copy(
+            src_ref=source, dst_ref=target, send_sem=send_sem.at[k_send], recv_sem=recv_sem.at[k_recv],
+            device_id=to, device_id_type=MESH,
+        )
+
     def to_relay(j):
-        me = {"group": group, "blk": blk}
-        return pltpu.make_async_remote_copy(
-            src_ref=own.at[near, rows_of(j)], dst_ref=relay.at[lax.rem(x, 2)],
-            send_sem=send_sem.at[near * 12 + 4 + j], recv_sem=recv_sem.at[24 + lax.rem(x, 2)],
-            device_id=relay_of(near, me, j), device_id_type=MESH,
-        )
+        return hop(own.at[near, rows_of(j)], relay.at[0], near * 12 + 4 + j, 24, at(x, j, z, near))
+
+    def pass_on():
+        return hop(relay.at[0], relay.at[1], 24, 25, pass_to)
 
     def from_relay(slot):
         holder = served(slot)
-        return pltpu.make_async_remote_copy(
-            src_ref=relay.at[slot], dst_ref=far.at[core, 1, rows_of(y)],
-            send_sem=send_sem.at[24 + slot], recv_sem=recv_sem.at[core * 12 + 4 + y],
-            device_id=device(holder["group"] + step(core), holder["blk"] + 2 * step(core)), device_id_type=MESH,
-        )
-
-    def relay_in(slot):
-        return pltpu.make_async_remote_copy(
-            src_ref=own.at[0, rows_of(0)], dst_ref=relay.at[slot],
-            send_sem=send_sem.at[24 + slot], recv_sem=recv_sem.at[24 + slot],
-            device_id=along(0), device_id_type=MESH,
-        )
+        to = device(holder["group"] + step(core), holder["blk"] + 2 * step(core))
+        return hop(relay.at[slot], far.at[core, 1, rows_of(y)], 24 + slot, core * 12 + 4 + y, to)
 
     @pl.when(edge)
     def _():
@@ -160,16 +158,14 @@
 
     scale = jnp.exp(jnp.full((1, rows), temp_ref[0], F32))
     shift = bias_ref[0]
-    gain = scale * (1.0 / math.sqrt(4 * rows))
 
     def pair(products):
-        logits = scale * products + shift
+        logits = scale[:, : products.shape[1]] * products + shift
         small = jnp.exp(-jnp.abs(logits))
         total = 1.0 + small
         log1p = jnp.where(total == 1.0, small, jnp.log(total) * (small / (total - 1.0)))
         weights = jnp.where(logits >= 0, 1.0, small) / total
-        losses = jnp.maximum(logits, 0.0) + log1p
-        return losses[:, :128] + losses[:, 128:], weights * gain
+        return jnp.maximum(logits, 0.0) + log1p, weights
 
     def held(kind):
         return own_high[kind], own_low[kind]
@@ -183,9 +179,17 @@
     lax.fori_loop(0, PARTS, own_part, 0)
 
     losses, weights = pair(dot3(held(1), held(0), NT))
-    loss_part[0] = losses
+    loss_part[0] = losses[:, :128] + losses[:, 128:]
     grad[0] = dot3(split(weights), held(0), NN)
     grad[1] = dot3(split(weights.T), held(1), NN)
+
+    def meet_half(kind, leg, half):
+        lines = rows // 2
+        other = split(far[kind, leg, half * lines : (half + 1) * lines])
+        mine = 1 - kind
+        losses, weights = pair(dot3((own_high[mine], own_low[mine]), other, NT))
+        loss_part[kind] += losses
+        grad[kind] += dot3(split(weights), other, NN)
 
     def meet(kind, leg):
         def part_of(j, _):
@@ -197,7 +201,7 @@
         other = (high[...], low[...])
         mine = 1 - kind
         losses, weights = pair(dot3((own_high[mine], own_low[mine]), other, NT))
-        loss_part[kind] += losses
+        loss_part[kind] += losses[:, :128] + losses[:, 128:]
         grad[kind] += dot3(split(weights), other, NN)
 
     loss_part[1] = jnp.zeros_like(loss_part[1])
@@ -228,14 +232,23 @@
             take1(0, j)
             take1(1, j)
 
+    hop(relay.at[0], relay.at[0], 24, 24, along(0)).wait_recv()
+
+    @pl.when(inner)
+    def _():
+        from_relay(0).start()
+
+    @pl.when(outer)
+    def _():
+        pass_on().start()
+
     take0(0)
     take0(1)
 
-    @pl.when(relays)
-    def _():
-        for slot in range(2):
-            relay_in(slot).wait_recv()
-            from_relay(slot).start()
+    @pl.when(inner)
+    def _():
+        hop(relay.at[1], relay.at[1], 25, 25, along(0)).wait_recv()
+        from_relay(1).start()
 
     take1_ordinary(0)
     take0(2)
@@ -253,45 +266,30 @@
             take1(late, j)
 
     meet(late, 1)
-    for j in range(PARTS):
-        leg2(near, j).wait_recv()
-    meet(near, 2)
+    for half in range(2):
+        for kind in (near, late):
+            for j in range(half * PARTS // 2, (half + 1) * PARTS // 2):
+                leg2(kind, j).wait_recv()
+            meet_half(kind, 2, half)
 
     write_x = pltpu.make_async_copy(grad.at[0], gx_hbm, out_sem.at[0])
     write_y = pltpu.make_async_copy(grad.at[1], gy_hbm, out_sem.at[1])
-
-    @pl.when(first)
-    def _():
-        write_y.start()
-
-    @pl.when(jnp.logical_not(first))
-    def _():
-        write_x.start()
-
-    for j in range(PARTS):
-        leg2(late, j).wait_recv()
-    meet(late, 2)
-
-    @pl.when(first)
-    def _():
-        write_x.start()
-
-    @pl.when(jnp.logical_not(first))
-    def _():
-        write_y.start()
+    write_x.start()
+    write_y.start()
 
     loss_ref[...] = lax.dot_general(
         jnp.ones((8, 128), F32), loss_part[0], NT, precision=lax.Precision.HIGHEST, preferred_element_type=F32
-    ) * (1.0 / (4 * rows))
+    )
 
     for kind in range(2):
         for j in range(PARTS):
             leg1(kind, j).wait_send()
             leg2(kind, j).wait_send()
 
-    @pl.when(relays)
-    def _():
-        from_relay(0).wait_send()
+    from_relay(0).wait_send()
+
+    @pl.when(inner)
+    def _():
         from_relay(1).wait_send()
 
     write_x.wait()
@@ -306,7 +304,7 @@
     in_hbm = pl.BlockSpec(memory_space=pltpu.HBM)
     scalar = pl.BlockSpec(memory_space=pltpu.SMEM)
     whole = jax.ShapeDtypeStruct((rows, width), F32)
-    row_loss, grad_x, grad_y = pl.pallas_call(
+    losses, grad_x, grad_y = pl.pallas_call(
         kernel,
         out_shape=(jax.ShapeDtypeStruct((8, rows), F32), whole, whole),
         in_specs=[scalar, scalar, in_hbm, in_hbm],
@@ -327,7 +325,8 @@
         ),
         name="pair_tiles",
     )(log_temp, bias, images, held_text)
-    return row_loss[0], grad_x, grad_y
+    gain = jnp.exp(log_temp) * (1.0 / math.sqrt(4 * rows))
+    return losses[0] * (1.0 / (4 * rows)), grad_x * gain, grad_y * gain
 
 
 def solution(mesh):

time: 136 us -> 112 us (0.82)
  the two profiles are of different devices: /device:TPU:32 before, /device:TPU:47 now
where the time goes in v3:
time: 112 us
  Pallas kernels  105 us (94%)
  other arithmetic  4.44 us (4%)
  between operations  1.97 us (2%)
    pallas_call x1, Pallas kernels, body(): pl.pallas_call(kernel, out_shape=(jax.ShapeDtypeStruct((8, rows), F32), w...  105 us
    mul x2, other arithmetic, body(): return (losses[0] * (1.0 / (4 * rows)), grad_x * gain, grad_y * gain)  4.44 us

profile of v3, /device:TPU:47, one launch (start us, length us, event | category | flops | bytes accessed | tf_op | source)
XLA Modules:
  0.0 111.9 jit_solution(767759592679956413)
XLA Ops:
  2.0 105.5 %pair_tiles.1 = (f32[8,256]{1,0:T(8,128)}, f32[256,1152]{1,0:T(8,128)}, f32[256,1152]{1,0:T(8,128)}) custom-call(f32[1]{0:T(128)S(6)} %copy.7.temp_ref, f32[1]{0:T(128)S(6)} %copy.8.bias_ref, f32[256,1152]{1,0:T(8,128)} %x_hbm.1, f32[256,1152]{1,0:T(8,128)} %y_hbm.1), custom_call_target="tpu_custom_call" | custom-call | tf_op jit(solution)/shard_map/pair_tiles/pallas_call | solution.py:307
  107.5 1.3 %slice_multiply_fusion = f32[1,256]{1,0:T(1,128)} fusion(f32[8,256]{1,0:T(8,128)} %get-tuple-element.6), kind=kLoop, calls=%fused_computation.2 | loop fusion | flops 256 | bytes 2048 | tf_op jit(solution)/shard_map/mul | solution.py:329
  108.7 3.2 %broadcast_multiply_fusion = (f32[256,1152]{1,0:T(8,128)}, f32[256,1152]{1,0:T(8,128)}) fusion(f32[256,1152]{1,0:T(8,128)} %get-tuple-element.8, f32[]{:T(128)} %bitcast.1, f32[256,1152]{1,0:T(8,128)} %get-tuple-element.7), kind=kLoop, calls=%fused_computation | loop fusion | flops 589824 | bytes 4718596 | tf_op jit(solution)/shard_map/mul | solution.py:329

commit v4 on v3

--- a/solution.py
+++ b/solution.py
@@ -37,7 +37,7 @@
 def kernel(
     temp_ref, bias_ref, x_hbm, y_hbm, loss_ref, gx_hbm, gy_hbm,
     own, own_high, own_low, far, high, low, grad, relay, loss_part,
-    load_sem, send_sem, recv_sem, out_sem,
+    load_sem, send_sem, recv_sem, out_sem, go_sem,
 ):
     rows = own.shape[1]
     part = rows // PARTS
@@ -52,6 +52,9 @@
     inner = (x == 1) | (x == 2)
     outer = jnp.logical_not(inner)
 
+    low_z = z < 8
+    blk_start, blk_end = low_z & (blk == 0), low_z & (blk == 31)
+
     def step(kind):
         return 1 - 2 * kind
 
@@ -87,22 +90,32 @@
     def signal(to):
         pl.semaphore_signal(barrier, inc=1, device_id=to, device_id_type=MESH)
 
-    signal(along(0))
+    def receiver(slot):
+        holder = served(slot)
+        return device(holder["group"] + step(core), holder["blk"] + 2 * step(core))
+
     signal(along(1))
 
     @pl.when(jnp.logical_not(first))
     def _():
         signal(across(1))
 
-    @pl.when(jnp.logical_not(last))
+    @pl.when(jnp.logical_not(blk_end))
+    def _():
+        signal(along(0))
+
+    @pl.when(jnp.logical_not(blk_end | last))
     def _():
         signal(across(0))
 
-    @pl.when(edge)
-    def _():
+    def each_late_relay(use):
         holder = device(group - step(late), blk - 2 * step(late))
         for j in range(PARTS):
-            signal(relay_of(late, holder, j))
+            use(relay_of(late, holder, j), holder)
+
+    @pl.when(edge & low_z)
+    def _():
+        each_late_relay(lambda to, holder: signal(to))
 
     signal(served(0))
 
@@ -110,7 +123,34 @@
     def _():
         signal(pass_from)
 
-    pl.semaphore_wait(barrier, jnp.where(edge, PARTS + 3, 4) + jnp.where(inner, 2, 1))
+    @pl.when(inner & low_z)
+    def _():
+        signal(receiver(0))
+        signal(receiver(1))
+
+    senders = jnp.where(edge, PARTS + 3, 4) - jnp.where(blk_start, jnp.where(first, 1, 2), 0)
+    passing = jnp.where(inner, jnp.where(low_z, 0, 2), 1)
+    pl.semaphore_wait(barrier, senders + passing + jnp.where(edge & jnp.logical_not(low_z), PARTS, 0))
+
+    def go(k, to):
+        pl.semaphore_signal(go_sem.at[k], inc=1, device_id=to, device_id_type=MESH)
+
+    @pl.when(edge & jnp.logical_not(low_z))
+    def _():
+        def tell(to, holder):
+            x_from = lax.rem(holder["blk"], 4)
+            go(jnp.where((x_from == 0) | (x_from == 3), 1, 0), to)
+
+        each_late_relay(tell)
+
+    @pl.when(blk_end)
+    def _():
+        go(2, along(0))
+
+    @pl.when(blk_end & jnp.logical_not(last))
+    def _():
+        go(3, across(0))
+
     load_y.wait()
     load_x.wait()
 
@@ -143,18 +183,21 @@
         return hop(relay.at[0], relay.at[1], 24, 25, pass_to)
 
     def from_relay(slot):
-        holder = served(slot)
-        to = device(holder["group"] + step(core), holder["blk"] + 2 * step(core))
-        return hop(relay.at[slot], far.at[core, 1, rows_of(y)], 24 + slot, core * 12 + 4 + y, to)
+        return hop(relay.at[slot], far.at[core, 1, rows_of(y)], 24 + slot, core * 12 + 4 + y, receiver(slot))
 
     @pl.when(edge)
     def _():
         for j in range(PARTS):
             to_relay(j).start()
 
-    for j in range(2):
-        for kind in range(2):
-            leg0(kind, j).start()
+    leg0(0, 0).start()
+
+    @pl.when(jnp.logical_not(blk_start))
+    def _():
+        leg0(1, 0).start()
+        leg0(1, 1).start()
+
+    leg0(0, 1).start()
 
     scale = jnp.exp(jnp.full((1, rows), temp_ref[0], F32))
     shift = bias_ref[0]
@@ -232,18 +275,38 @@
             take1(0, j)
             take1(1, j)
 
+    @pl.when(blk_start)
+    def _():
+        pl.semaphore_wait(go_sem.at[2], 1)
+        leg0(1, 0).start()
+        leg0(1, 1).start()
+
+    @pl.when(blk_start & jnp.logical_not(first))
+    def _():
+        pl.semaphore_wait(go_sem.at[3], 1)
+
     hop(relay.at[0], relay.at[0], 24, 24, along(0)).wait_recv()
 
-    @pl.when(inner)
+    @pl.when(outer)
+    def _():
+        pass_on().start()
+
+    @pl.when(inner & jnp.logical_not(low_z))
     def _():
         from_relay(0).start()
 
-    @pl.when(outer)
-    def _():
-        pass_on().start()
-
     take0(0)
+
+    @pl.when(inner & low_z)
+    def _():
+        pl.semaphore_wait(go_sem.at[0], 1)
+        from_relay(0).start()
+
     take0(1)
+
+    @pl.when(inner & low_z)
+    def _():
+        pl.semaphore_wait(go_sem.at[1], 1)
 
     @pl.when(inner)
     def _():
@@ -266,16 +329,35 @@
             take1(late, j)
 
     meet(late, 1)
-    for half in range(2):
-        for kind in (near, late):
-            for j in range(half * PARTS // 2, (half + 1) * PARTS // 2):
-                leg2(kind, j).wait_recv()
-            meet_half(kind, 2, half)
-
     write_x = pltpu.make_async_copy(grad.at[0], gx_hbm, out_sem.at[0])
     write_y = pltpu.make_async_copy(grad.at[1], gy_hbm, out_sem.at[1])
-    write_x.start()
-    write_y.start()
+
+    def last_half(kind, half):
+        for j in range(half * PARTS // 2, (half + 1) * PARTS // 2):
+            leg2(kind, j).wait_recv()
+        meet_half(kind, 2, half)
+
+    last_half(near, 0)
+    last_half(late, 0)
+    last_half(near, 1)
+
+    @pl.when(first)
+    def _():
+        write_y.start()
+
+    @pl.when(jnp.logical_not(first))
+    def _():
+        write_x.start()
+
+    last_half(late, 1)
+
+    @pl.when(first)
+    def _():
+        write_x.start()
+
+    @pl.when(jnp.logical_not(first))
+    def _():
+        write_y.start()
 
     loss_ref[...] = lax.dot_general(
         jnp.ones((8, 128), F32), loss_part[0], NT, precision=lax.Precision.HIGHEST, preferred_element_type=F32
@@ -319,9 +401,10 @@
             pltpu.SemaphoreType.DMA((26,)),
             pltpu.SemaphoreType.DMA((26,)),
             pltpu.SemaphoreType.DMA((2,)),
+            pltpu.SemaphoreType.REGULAR((4,)),
         ],
         compiler_params=pltpu.CompilerParams(
-            collective_id=0, has_side_effects=True, vmem_limit_bytes=60 * 1024 * 1024
+            collective_id=0, has_side_effects=True, vmem_limit_bytes=51 * 1024 * 1024
         ),
         name="pair_tiles",
     )(log_temp, bias, images, held_text)

time: 112 us -> 107 us (0.955)
  the two profiles are of different devices: /device:TPU:47 before, /device:TPU:8 now
where the time goes in v4:
time: 107 us
  Pallas kernels  103 us (96%)
  other arithmetic  2.12 us (2%)
  between operations  1.97 us (2%)
    pallas_call x1, Pallas kernels, body(): pl.pallas_call(kernel, out_shape=(jax.ShapeDtypeStruct((8, rows), F32), w...  103 us

profile of v4, /device:TPU:8, one launch (start us, length us, event | category | flops | bytes accessed | tf_op | source)
XLA Modules:
  0.0 107.2 jit_solution(10564199208584538970)
XLA Ops:
  2.0 103.1 %pair_tiles.1 = (f32[8,256]{1,0:T(8,128)S(1)}, f32[256,1152]{1,0:T(8,128)S(1)}, f32[256,1152]{1,0:T(8,128)S(1)}) custom-call(f32[1]{0:T(128)S(6)} %copy.7.temp_ref, f32[1]{0:T(128)S(6)} %copy.8.bias_ref, f32[256,1152]{1,0:T(8,128)} %x_hbm.1, f32[256,1152]{1,0:T(8,128)} %y_hbm.1), custom_call_target="tpu_custom_call" | custom-call | tf_op jit(solution)/shard_map/pair_tiles/pallas_call | solution.py:389
  105.1 0.6 slice_multiply_fusion
  105.7 1.6 %broadcast_multiply_fusion = (f32[256,1152]{1,0:T(8,128)}, f32[256,1152]{1,0:T(8,128)}) fusion(f32[256,1152]{1,0:T(8,128)S(1)} %get-tuple-element.8, f32[]{:T(128)} %bitcast.1, f32[256,1152]{1,0:T(8,128)S(1)} %get-tuple-element.7), kind=kLoop, calls=%fused_computation | loop fusion | flops 589824 | bytes 4718596 | tf_op jit(solution)/shard_map/mul | solution.py:412

commit v5 on v4

--- a/solution.py
+++ b/solution.py
@@ -51,6 +51,7 @@
     late = 1 - near
     inner = (x == 1) | (x == 2)
     outer = jnp.logical_not(inner)
+    hub = x == jnp.where(core == 0, 2, 1)
 
     low_z = z < 8
     blk_start, blk_end = low_z & (blk == 0), low_z & (blk == 31)
@@ -64,18 +65,20 @@
     def across(kind):
         return device(group + step(kind), blk + step(kind))
 
-    def ring(x_from):
-        return jnp.where(x_from == 0, 2, jnp.where(x_from == 3, 1, x_from))
+    def ring(x_from, kind):
+        return jnp.where((x_from == 0) | (x_from == 3), jnp.where(kind == 0, 2, 1), x_from)
+
+    def slot_of(x_from):
+        return jnp.where(x_from == 0, 1, jnp.where(x_from == 3, 2, 0))
 
     def relay_of(kind, holder, j):
         z_from = (holder["group"] // 8) * 8 + holder["blk"] // 4
-        return at(ring(lax.rem(holder["blk"], 4)), j, z_from, kind)
+        return at(ring(lax.rem(holder["blk"], 4), kind), j, z_from, kind)
 
     def served(slot):
-        x_from = x if slot == 0 else jnp.where(x == 2, 0, 3)
-        return at(x_from, jnp.where(core == 0, 3, 0), z, 1 - core)
-
-    pass_to, pass_from = at(ring(x), y, z, core), at(jnp.where(x == 2, 0, 3), y, z, core)
+        return at((x, 0, 3)[slot], jnp.where(core == 0, 3, 0), z, 1 - core)
+
+    pass_to = at(ring(x, core), y, z, core)
 
     def rows_of(j):
         return pl.ds(pl.multiple_of(j * part, part), part)
@@ -92,7 +95,7 @@
 
     def receiver(slot):
         holder = served(slot)
-        return device(holder["group"] + step(core), holder["blk"] + 2 * step(core))
+        return device(holder["group"] + step(core), holder["blk"] + 3 * step(core))
 
     signal(along(1))
 
@@ -109,7 +112,7 @@
         signal(across(0))
 
     def each_late_relay(use):
-        holder = device(group - step(late), blk - 2 * step(late))
+        holder = device(group - step(late), blk - 3 * step(late))
         for j in range(PARTS):
             use(relay_of(late, holder, j), holder)
 
@@ -119,17 +122,22 @@
 
     signal(served(0))
 
-    @pl.when(inner)
-    def _():
-        signal(pass_from)
+    @pl.when(hub)
+    def _():
+        signal(at(0, y, z, core))
+        signal(at(3, y, z, core))
 
     @pl.when(inner & low_z)
     def _():
         signal(receiver(0))
+
+    @pl.when(hub & low_z)
+    def _():
         signal(receiver(1))
+        signal(receiver(2))
 
     senders = jnp.where(edge, PARTS + 3, 4) - jnp.where(blk_start, jnp.where(first, 1, 2), 0)
-    passing = jnp.where(inner, jnp.where(low_z, 0, 2), 1)
+    passing = jnp.where(outer, 1, jnp.where(low_z, 0, jnp.where(hub, 3, 1)))
     pl.semaphore_wait(barrier, senders + passing + jnp.where(edge & jnp.logical_not(low_z), PARTS, 0))
 
     def go(k, to):
@@ -138,18 +146,17 @@
     @pl.when(edge & jnp.logical_not(low_z))
     def _():
         def tell(to, holder):
-            x_from = lax.rem(holder["blk"], 4)
-            go(jnp.where((x_from == 0) | (x_from == 3), 1, 0), to)
+            go(slot_of(lax.rem(holder["blk"], 4)), to)
 
         each_late_relay(tell)
 
     @pl.when(blk_end)
     def _():
-        go(2, along(0))
+        go(3, along(0))
 
     @pl.when(blk_end & jnp.logical_not(last))
     def _():
-        go(3, across(0))
+        go(4, across(0))
 
     load_y.wait()
     load_x.wait()
@@ -168,7 +175,8 @@
         return copy(kind, 1, j, far.at[kind, 0, rows_of(j)], across(kind))
 
     def leg2(kind, j):
-        return copy(kind, 2, j, far.at[kind, 1, rows_of(j)], along(kind))
+        back = edge & (late == kind)
+        return copy(kind, 2, j, far.at[kind, 1, rows_of(j)], device(group, blk + jnp.where(back, -step(kind), step(kind))))
 
     def hop(source, target, k_send, k_recv, to):
         return pltpu.make_async_remote_copy(
@@ -180,7 +188,7 @@
         return hop(own.at[near, rows_of(j)], relay.at[0], near * 12 + 4 + j, 24, at(x, j, z, near))
 
     def pass_on():
-        return hop(relay.at[0], relay.at[1], 24, 25, pass_to)
+        return hop(relay.at[0], relay.at[slot_of(x)], 24, 24 + slot_of(x), pass_to)
 
     def from_relay(slot):
         return hop(relay.at[slot], far.at[core, 1, rows_of(y)], 24 + slot, core * 12 + 4 + y, receiver(slot))
@@ -277,13 +285,13 @@
 
     @pl.when(blk_start)
     def _():
-        pl.semaphore_wait(go_sem.at[2], 1)
+        pl.semaphore_wait(go_sem.at[3], 1)
         leg0(1, 0).start()
         leg0(1, 1).start()
 
     @pl.when(blk_start & jnp.logical_not(first))
     def _():
-        pl.semaphore_wait(go_sem.at[3], 1)
+        pl.semaphore_wait(go_sem.at[4], 1)
 
     hop(relay.at[0], relay.at[0], 24, 24, along(0)).wait_recv()
 
@@ -304,14 +312,15 @@
 
     take0(1)
 
-    @pl.when(inner & low_z)
-    def _():
-        pl.semaphore_wait(go_sem.at[1], 1)
-
-    @pl.when(inner)
-    def _():
-        hop(relay.at[1], relay.at[1], 25, 25, along(0)).wait_recv()
-        from_relay(1).start()
+    for slot in (1, 2):
+        @pl.when(hub & low_z)
+        def _():
+            pl.semaphore_wait(go_sem.at[slot], 1)
+
+        @pl.when(hub)
+        def _():
+            hop(relay.at[slot], relay.at[slot], 24 + slot, 24 + slot, along(0)).wait_recv()
+            from_relay(slot).start()
 
     take1_ordinary(0)
     take0(2)
@@ -370,9 +379,10 @@
 
     from_relay(0).wait_send()
 
-    @pl.when(inner)
+    @pl.when(hub)
     def _():
         from_relay(1).wait_send()
+        from_relay(2).wait_send()
 
     write_x.wait()
     write_y.wait()
@@ -395,13 +405,13 @@
             pieces, halves, halves,
             pltpu.VMEM((2, 3, rows, width), F32),
             half, half, pieces,
-            pltpu.VMEM((2, rows // PARTS, width), F32),
+            pltpu.VMEM((3, rows // PARTS, width), F32),
             pltpu.VMEM((2, rows, 128), F32),
             pltpu.SemaphoreType.DMA((2,)),
-            pltpu.SemaphoreType.DMA((26,)),
-            pltpu.SemaphoreType.DMA((26,)),
+            pltpu.SemaphoreType.DMA((27,)),
+            pltpu.SemaphoreType.DMA((27,)),
             pltpu.SemaphoreType.DMA((2,)),
-            pltpu.SemaphoreType.REGULAR((4,)),
+            pltpu.SemaphoreType.REGULAR((5,)),
         ],
         compiler_params=pltpu.CompilerParams(
             collective_id=0, has_side_effects=True, vmem_limit_bytes=51 * 1024 * 1024

time: 107 us -> 104 us (0.972)
  the two profiles are of different devices: /device:TPU:8 before, /device:TPU:25 now
where the time goes in v5:
time: 104 us
  Pallas kernels  100 us (96%)
  other arithmetic  2.12 us (2%)
  between operations  1.97 us (2%)
    pallas_call x1, Pallas kernels, body(): pl.pallas_call(kernel, out_shape=(jax.ShapeDtypeStruct((8, rows), F32), w...  100 us
    mul x2, other arithmetic, body(): return (losses[0] * (1.0 / (4 * rows)), grad_x * gain, grad_y * gain)  2.12 us

profile of v5, /device:TPU:25, one launch (start us, length us, event | category | flops | bytes accessed | tf_op | source)
XLA Modules:
  0.0 104.1 jit_solution(6763456482641569538)
XLA Ops:
  2.0 100.0 %pair_tiles.1 = (f32[8,256]{1,0:T(8,128)S(1)}, f32[256,1152]{1,0:T(8,128)S(1)}, f32[256,1152]{1,0:T(8,128)S(1)}) custom-call(f32[1]{0:T(128)S(6)} %copy.7.temp_ref, f32[1]{0:T(128)S(6)} %copy.8.bias_ref, f32[256,1152]{1,0:T(8,128)} %x_hbm.1, f32[256,1152]{1,0:T(8,128)} %y_hbm.1), custom_call_target="tpu_custom_call" | custom-call | tf_op jit(solution)/shard_map/pair_tiles/pallas_call | solution.py:399
  102.0 0.6 slice_multiply_fusion
  102.6 1.6 %broadcast_multiply_fusion = (f32[256,1152]{1,0:T(8,128)}, f32[256,1152]{1,0:T(8,128)}) fusion(f32[256,1152]{1,0:T(8,128)S(1)} %get-tuple-element.8, f32[]{:T(128)} %bitcast.1, f32[256,1152]{1,0:T(8,128)S(1)} %get-tuple-element.7), kind=kLoop, calls=%fused_computation | loop fusion | flops 589824 | bytes 4718596 | tf_op jit(solution)/shard_map/mul | solution.py:422

commit v6 on v5

--- a/solution.py
+++ b/solution.py
@@ -23,6 +23,8 @@
     def one(p, q):
         return lax.dot_general(p, q, dims, preferred_element_type=F32)
 
+    if dims == NN:
+        return one(jnp.concatenate([a[0], a[0], a[1]], axis=1), jnp.concatenate([b[0], b[1], b[0]], axis=0))
     return one(a[0], b[0]) + (one(a[0], b[1]) + one(a[1], b[0]))
 
 
@@ -47,7 +49,7 @@
     first = lax.rem(group, 8) == 0
     last = lax.rem(group, 8) == 7
     edge = first | last
-    near = jnp.where(first, 1, 0)
+    near = jnp.where(first | ((blk == 0) & jnp.logical_not(last)), 1, 0)
     late = 1 - near
     inner = (x == 1) | (x == 2)
     outer = jnp.logical_not(inner)
@@ -216,7 +218,7 @@
         total = 1.0 + small
         log1p = jnp.where(total == 1.0, small, jnp.log(total) * (small / (total - 1.0)))
         weights = jnp.where(logits >= 0, 1.0, small) / total
-        return jnp.maximum(logits, 0.0) + log1p, weights
+        return jnp.maximum(logits, 0.0) + log1p, weights * scale[:, : products.shape[1]]
 
     def held(kind):
         return own_high[kind], own_low[kind]
@@ -310,8 +312,6 @@
         pl.semaphore_wait(go_sem.at[0], 1)
         from_relay(0).start()
 
-    take0(1)
-
     for slot in (1, 2):
         @pl.when(hub & low_z)
         def _():
@@ -321,6 +321,8 @@
         def _():
             hop(relay.at[slot], relay.at[slot], 24 + slot, 24 + slot, along(0)).wait_recv()
             from_relay(slot).start()
+
+    take0(1)
 
     take1_ordinary(0)
     take0(2)
@@ -346,25 +348,26 @@
             leg2(kind, j).wait_recv()
         meet_half(kind, 2, half)
 
-    last_half(near, 0)
-    last_half(late, 0)
-    last_half(near, 1)
-
-    @pl.when(first)
+    sooner = jnp.where(blk == 0, 1, near)
+    last_half(sooner, 0)
+    last_half(1 - sooner, 0)
+    last_half(sooner, 1)
+
+    @pl.when(sooner == 1)
     def _():
         write_y.start()
 
-    @pl.when(jnp.logical_not(first))
+    @pl.when(sooner == 0)
     def _():
         write_x.start()
 
-    last_half(late, 1)
-
-    @pl.when(first)
+    last_half(1 - sooner, 1)
+
+    @pl.when(sooner == 1)
     def _():
         write_x.start()
 
-    @pl.when(jnp.logical_not(first))
+    @pl.when(sooner == 0)
     def _():
         write_y.start()
 
@@ -418,7 +421,7 @@
         ),
         name="pair_tiles",
     )(log_temp, bias, images, held_text)
-    gain = jnp.exp(log_temp) * (1.0 / math.sqrt(4 * rows))
+    gain = 1.0 / math.sqrt(4 * rows)
     return losses[0] * (1.0 / (4 * rows)), grad_x * gain, grad_y * gain
 
 

time: 104 us -> 106 us (1.019)
  Pallas kernels: 100 us -> 102 us
    pallas_call x1, Pallas kernels: 100 us -> 102 us  [body(): pl.pallas_call(kernel, out_shape=(jax.ShapeDtypeStruct((8, rows), F32), w...]
where the time goes in v6:
time: 106 us
  Pallas kernels  102 us (96%)
  other arithmetic  2.12 us (2%)
  between operations  1.93 us (2%)
    pallas_call x1, Pallas kernels, body(): pl.pallas_call(kernel, out_shape=(jax.ShapeDtypeStruct((8, rows), F32), w...  102 us

profile of v6, /device:TPU:25, one launch (start us, length us, event | category | flops | bytes accessed | tf_op | source)
XLA Modules:
  0.0 105.6 jit_solution(10806055674518745141)
XLA Ops:
  1.9 101.6 %pair_tiles.1 = (f32[8,256]{1,0:T(8,128)S(1)}, f32[256,1152]{1,0:T(8,128)S(1)}, f32[256,1152]{1,0:T(8,128)S(1)}) custom-call(f32[1]{0:T(128)S(6)} %copy.7.temp_ref, f32[1]{0:T(128)S(6)} %copy.8.bias_ref, f32[256,1152]{1,0:T(8,128)} %x_hbm.1, f32[256,1152]{1,0:T(8,128)} %y_hbm.1), custom_call_target="tpu_custom_call" | custom-call | tf_op jit(solution)/shard_map/pair_tiles/pallas_call | solution.py:402
  103.5 0.6 slice_multiply_fusion
  104.1 1.6 %broadcast_multiply_fusion = (f32[256,1152]{1,0:T(8,128)}, f32[256,1152]{1,0:T(8,128)}) fusion(f32[256,1152]{1,0:T(8,128)S(1)} %get-tuple-element.8, f32[256,1152]{1,0:T(8,128)S(1)} %get-tuple-element.7), kind=kLoop, calls=%fused_computation | loop fusion | flops 589824 | bytes 4718592 | tf_op jit(solution)/shard_map/mul | solution.py:425

commit v7 on v6

--- a/solution.py
+++ b/solution.py
@@ -348,26 +348,25 @@
             leg2(kind, j).wait_recv()
         meet_half(kind, 2, half)
 
-    sooner = jnp.where(blk == 0, 1, near)
-    last_half(sooner, 0)
-    last_half(1 - sooner, 0)
-    last_half(sooner, 1)
-
-    @pl.when(sooner == 1)
+    last_half(near, 0)
+    last_half(late, 0)
+    last_half(near, 1)
+
+    @pl.when(near == 1)
     def _():
         write_y.start()
 
-    @pl.when(sooner == 0)
+    @pl.when(near == 0)
     def _():
         write_x.start()
 
-    last_half(1 - sooner, 1)
-
-    @pl.when(sooner == 1)
+    last_half(late, 1)
+
+    @pl.when(near == 1)
     def _():
         write_x.start()
 
-    @pl.when(sooner == 0)
+    @pl.when(near == 0)
     def _():
         write_y.start()
 

time: 106 us -> 104 us (0.981)
  Pallas kernels: 102 us -> 99.9 us
    pallas_call x1, Pallas kernels: 102 us -> 99.9 us  [body(): pl.pallas_call(kernel, out_shape=(jax.ShapeDtypeStruct((8, rows), F32), w...]
where the time goes in v7:
time: 104 us
  Pallas kernels  99.9 us (96%)
  other arithmetic  2.12 us (2%)
  between operations  1.93 us (2%)
    pallas_call x1, Pallas kernels, body(): pl.pallas_call(kernel, out_shape=(jax.ShapeDtypeStruct((8, rows), F32), w...  99.9 us
    mul x2, other arithmetic, body(): return (losses[0] * (1.0 / (4 * rows)), grad_x * gain, grad_y * gain)  2.12 us

profile of v7, /device:TPU:25, one launch (start us, length us, event | category | flops | bytes accessed | tf_op | source)
XLA Modules:
  0.0 104.0 jit_solution(3841076294958802447)
XLA Ops:
  1.9 99.9 %pair_tiles.1 = (f32[8,256]{1,0:T(8,128)S(1)}, f32[256,1152]{1,0:T(8,128)S(1)}, f32[256,1152]{1,0:T(8,128)S(1)}) custom-call(f32[1]{0:T(128)S(6)} %copy.7.temp_ref, f32[1]{0:T(128)S(6)} %copy.8.bias_ref, f32[256,1152]{1,0:T(8,128)} %x_hbm.1, f32[256,1152]{1,0:T(8,128)} %y_hbm.1), custom_call_target="tpu_custom_call" | custom-call | tf_op jit(solution)/shard_map/pair_tiles/pallas_call | solution.py:401
  101.9 0.6 slice_multiply_fusion
  102.4 1.6 %broadcast_multiply_fusion = (f32[256,1152]{1,0:T(8,128)}, f32[256,1152]{1,0:T(8,128)}) fusion(f32[256,1152]{1,0:T(8,128)S(1)} %get-tuple-element.8, f32[256,1152]{1,0:T(8,128)S(1)} %get-tuple-element.7), kind=kLoop, calls=%fused_computation | loop fusion | flops 589824 | bytes 4718592 | tf_op jit(solution)/shard_map/mul | solution.py:424
